TPU v7x, 256 devices: a whole 4x4x8 slice. The times are simulated.
256 devices in a mesh: rx: 32 (over z, x_hi, core), tm: 8 (over y, x_lo).
Axes of the slice: x: 4 (x_hi: 2, x_lo: 2; x = x_hi * 2 + x_lo), y: 4, z: 8, core: 2. Of those that a mesh axis runs over, the one named last changes fastest.
Arguments:
- records: float32 [4096, 24576], P('rx', 'tm'), may hold values from -1000 to 1000, as said below
- source_block: int32 [2], replicated, may hold values from 0 to 63
- quality: int32 [4096], P('rx'), may hold values 0 or 1
Outputs:
- stacks: float32 [2, 64, 101, 4096], P(None, 'tm', None, 'rx')
Inputs may be any that keep to these rules, and one draw needn't show every extreme that they name: Noise records with channel and window gains.
All inputs are finite; a program needn't handle non-finite values. No bound on the sum of `quality` on one device may be relied on, other than what follows from the above.
Results may differ from a plain program's by a relative error of at most 0.0039.
Values may be sent and summed in bfloat16 or wider, within the bound.
A program may use at most 192 MiB of HBM per device.

v0:
```python
import math
import jax
import jax.numpy as jnp
from jax import lax
from jax.sharding import PartitionSpec as P

W = 1024
HALF = 50
LAGS = 101
SRC = 64
STEPS = 2


def broadcast(block, axis, owner):
    block = jnp.where(lax.axis_index(axis) == owner, block, jnp.zeros_like(block))
    return lax.psum(block, axis)


def whiten(records, quality):
    receivers = records.shape[0]
    samples = records.reshape(receivers, records.shape[1] // W, W)
    power = jnp.mean(samples * samples, axis=2, keepdims=True)
    return (samples * lax.rsqrt(power + 1e-06) * quality.astype(jnp.float32)[:, None, None]).astype(
        jnp.bfloat16
    )


def broadcast_block(whitened, block):
    per_device = whitened.shape[0]
    first_row = block * SRC
    owner = first_row // per_device
    offset = first_row - owner * per_device
    local_rows = lax.dynamic_slice_in_dim(whitened, offset, SRC, 0)
    return broadcast(local_rows, "rx", owner)


def lag_split():
    fine_shifts = math.isqrt(LAGS - 1) + 1
    coarse_shifts = -(-LAGS // fine_shifts)
    return (fine_shifts, coarse_shifts)


def source_stack(sources, fine_shifts):
    shifted = [
        jnp.pad(sources, ((0, 0), (0, 0), (offset, fine_shifts - offset)))
        for offset in range(fine_shifts)
    ]
    stacked = jnp.stack(shifted, 1)
    return stacked.reshape(sources.shape[0] * fine_shifts, -1)


def receiver_stack(whitened, fine_shifts, coarse_shifts):
    padded = jnp.pad(whitened, ((0, 0), (0, 0), (HALF, coarse_shifts * fine_shifts - HALF)))
    length = whitened.shape[2] + fine_shifts
    shifted = [
        padded[:, :, number * fine_shifts : number * fine_shifts + length]
        for number in range(coarse_shifts)
    ]
    stacked = jnp.stack(shifted, 1)
    return stacked.reshape(whitened.shape[0] * coarse_shifts, -1)


def lag_products(source_rows, receiver_rows, row_count, receivers, fine_shifts, coarse_shifts):
    products = lax.dot_general(
        source_rows, receiver_rows, (((1,), (1,)), ((), ())), preferred_element_type=jnp.float32
    )
    products = products.reshape(row_count, fine_shifts, receivers, coarse_shifts)
    products = jnp.transpose(products, (0, 3, 1, 2)).reshape(
        row_count, coarse_shifts * fine_shifts, receivers
    )
    return products[:, :LAGS, :]


def on_device(records, source_block, quality):
    receivers = records.shape[0]
    windows_here = records.shape[1] // W
    groups = lax.axis_size("tm")
    weight = 1.0 / math.sqrt(W * windows_here * groups)
    whitened = whiten(records, quality)
    fine_shifts, coarse_shifts = lag_split()
    sources = []
    for number in range(STEPS):
        sources.append(broadcast_block(whitened, source_block[number]))
    share_rows = SRC // groups
    receiver_rows = receiver_stack(whitened, fine_shifts, coarse_shifts)
    source_sets = [source_stack(block_rows, fine_shifts) for block_rows in sources]
    results = []
    for source_rows in source_sets:

        def step_term(first_row, row_count, source_rows=source_rows):
            return (
                lag_products(
                    source_rows, receiver_rows, row_count, receivers, fine_shifts, coarse_shifts
                )
                * weight
            )

        results.append(
            lax.psum_scatter(
                step_term(jnp.int32(0), share_rows * lax.axis_size("tm")),
                "tm",
                scatter_dimension=0,
                tiled=True,
            )
        )
    return jnp.stack(results, 0)


def solution(mesh):
    in_specs = (P("rx", "tm"), P(), P("rx"))
    out_specs = P(None, "tm", None, "rx")
    return jax.shard_map(
        on_device, mesh=mesh, in_specs=in_specs, out_specs=out_specs, check_vma=False
    )
```

profile of v0, /device:TPU:1, one launch (start us, length us, event | category | flops | bytes accessed | tf_op | source)
XLA Modules:
  0.0 485.6 jit_solution(4198167202444544092)
XLA Ops:
  6.5 0.0 all-reduce.26.cloned.1.call-start
  6.5 1.3 fusion.16
  9.1 1.9 copy.7
  11.0 0.2 multiply_reduce_fusion
  11.2 0.7 convert_element_type.41
  11.8 0.2 multiply_convert_fusion
  12.0 1.7 dynamic-slice_select_fusion.1
  13.7 0.0 all-reduce.26.cloned.1.call-update
  13.7 0.0 reduce-scatter.3.cloned.1.call-start
  13.8 1.2 bitcast_dynamic-update-slice_fusion.20
  15.0 1.1 bitcast_dynamic-update-slice_fusion.19
  16.1 1.1 bitcast_dynamic-update-slice_fusion.18
  17.2 1.1 bitcast_dynamic-update-slice_fusion.17
  18.2 1.1 bitcast_dynamic-update-slice_fusion.16
  19.3 1.2 bitcast_dynamic-update-slice_fusion.15
  20.5 1.0 bitcast_dynamic-update-slice_fusion.14
  21.5 1.1 bitcast_dynamic-update-slice_fusion.13
  22.5 1.1 bitcast_dynamic-update-slice_fusion.12
  23.7 1.1 bitcast_dynamic-update-slice_fusion.11
  24.7 266.0 %all-reduce.26.cloned.1.call-done = (bf16[64,3,1024]{0,2,1:T(8,128)(2,1)}, bf16[64,3,1024]{0,2,1:T(8,128)(2,1)}) async-done(((bf16[64,3,1024]{0,2,1:T(8,128)(2,1)}, bf16[64,3,1024]{0,2,1:T(8,128)(2,1)}), (bf16[64,3,1024]{0,2,1:T(8,128)(2,1)}, bf16[64,3,1024]{0,2,1:T(8,128)(2,1)})) %all-reduce.26.cloned.1.call-update) | async-done | bytes 786448 | tf_op jit(solution)/shard_map/psum | solution.py:16
  290.7 0.0 copy-start.1
  290.7 0.0 copy-start
  290.7 1.4 bitcast_dynamic-update-slice_fusion.31
  292.1 1.4 bitcast_dynamic-update-slice_fusion.30
  293.6 1.4 bitcast_dynamic-update-slice_fusion.29
  295.0 1.4 bitcast_dynamic-update-slice_fusion.28
  296.5 1.4 bitcast_dynamic-update-slice_fusion.27
  297.9 1.4 bitcast_dynamic-update-slice_fusion.26
  299.3 0.0 copy-done.1
  299.3 0.3 bitcast_dynamic-update-slice_fusion.25
  299.6 0.3 bitcast_dynamic-update-slice_fusion.24
  299.9 0.2 bitcast_dynamic-update-slice_fusion.23
  300.2 0.3 bitcast_dynamic-update-slice_fusion.22
  300.5 0.0 copy-done
  300.5 0.2 bitcast_dynamic-update-slice_fusion.10
  300.6 0.3 bitcast_dynamic-update-slice_fusion.9
  300.9 0.3 bitcast_dynamic-update-slice_fusion.8
  301.2 0.3 bitcast_dynamic-update-slice_fusion.7
  301.6 0.3 bitcast_dynamic-update-slice_fusion.6
  301.9 0.3 bitcast_dynamic-update-slice_fusion.5
  302.2 0.3 bitcast_dynamic-update-slice_fusion.4
  302.5 0.3 bitcast_dynamic-update-slice_fusion.3
  302.8 0.2 bitcast_dynamic-update-slice_fusion.2
  303.0 0.3 bitcast_dynamic-update-slice_fusion.1
  303.3 0.6 bitcast_dynamic-update-slice_fusion
  303.9 0.0 copy-start.2
  303.9 3.4 copy-done.2
  307.3 10.3 %fusion.6 = f32[64,10,11,128]{3,0,1,2:T(8,128)S(1)} fusion(bf16[128,10,3,1035]{0,3,2,1:T(8,128)(2,1)} %bitcast_dynamic-update-slice_fusion.11, bf16[64,11,3,1035]{0,3,2,1:T(8,128)(2,1)S(1)} %get-tuple-element.12), kind=kOutput, calls=%fused_computation.8 | convolution fusion | flops 5595955200 | bytes 15925120 | tf_op jit(solution)/shard_map/dot_general | solution.py:64
  317.6 0.3 copy.9
  317.9 2.1 slice_multiply_fusion.1
  320.0 0.0 reduce-scatter.3.cloned.1.call-update
  320.0 0.0 reduce-scatter.5.cloned.1.call-start
  320.1 12.5 %fusion.11 = f32[64,10,11,128]{3,0,1,2:T(8,128)S(1)} fusion(bf16[128,10,3,1035]{0,3,2,1:T(8,128)(2,1)} %bitcast_dynamic-update-slice_fusion.11, bf16[64,11,3,1035]{0,3,2,1:T(8,128)(2,1)} %copy-done.2), kind=kOutput, calls=%fused_computation.9 | convolution fusion | flops 5595955200 | bytes 15925120 | tf_op jit(solution)/shard_map/dot_general | solution.py:64
  332.6 0.3 copy.11
  332.9 2.1 slice_multiply_fusion
  334.9 0.0 reduce-scatter.5.cloned.1.call-update
  335.0 61.6 %reduce-scatter.3.cloned.1.call-done = f32[8,101,128]{2,0,1:T(8,128)} async-done(((f32[64,101,128]{2,0,1:T(8,128)}), f32[8,101,128]{2,0,1:T(8,128)}) %reduce-scatter.3.cloned.1.call-update) | async-done | bytes 413712 | tf_op jit(solution)/shard_map/reduce_scatter | solution.py:99
  396.5 80.4 %reduce-scatter.5.cloned.1.call-done = f32[8,101,128]{2,0,1:T(8,128)} async-done(((f32[64,101,128]{2,0,1:T(8,128)}), f32[8,101,128]{2,0,1:T(8,128)}) %reduce-scatter.5.cloned.1.call-update) | async-done | bytes 413712 | tf_op jit(solution)/shard_map/reduce_scatter | solution.py:99
  477.0 2.1 pad_maximum_fusion
  (1 shorter events, 0.0 us)
Async XLA Ops:
  6.5 284.2 %all-reduce.26.cloned.1.call-start = ((), (), s32[]{:S(2)}) async-start(), calls=%async_computation.4 | async-start | bytes 3145728 | tf_op jit(solution)/shard_map/psum | solution.py:16
  13.7 382.8 %reduce-scatter.3.cloned.1.call-start = ((), (), s32[]{:S(2)}) async-start(), calls=%async_computation.2 | async-start | bytes 3723264 | tf_op jit(solution)/shard_map/reduce_scatter | solution.py:99
  290.7 8.6 %copy-start.1 = (bf16[64,3,1024]{0,2,1:T(8,128)(2,1)S(1)}, bf16[64,3,1024]{0,2,1:T(8,128)(2,1)}, u32[]{:S(2)}) copy-start(bf16[64,3,1024]{0,2,1:T(8,128)(2,1)} %get-tuple-element.6) | copy-start | bytes 1179652
  290.7 9.7 %copy-start = (bf16[64,3,1024]{0,2,1:T(8,128)(2,1)S(1)}, bf16[64,3,1024]{0,2,1:T(8,128)(2,1)}, u32[]{:S(2)}) copy-start(bf16[64,3,1024]{0,2,1:T(8,128)(2,1)} %get-tuple-element.5) | copy-start | bytes 1179652
  303.9 3.4 copy-start.2
  320.0 156.9 %reduce-scatter.5.cloned.1.call-start = ((), (), s32[]{:S(2)}) async-start(), calls=%async_computation.3 | async-start | bytes 3723264 | tf_op jit(solution)/shard_map/reduce_scatter | solution.py:99
Sparse Core Ops, SparseCore 0:
  13.9 276.8 all-reduce.25
  320.1 76.3 reduce-scatter.2
  399.3 77.6 reduce-scatter.4
where the time goes:
time: 486 us
  waiting for transfers between devices  408 us (84%)
  local copies, waits for them, and re-layouts  31.1 us (6%)
  matrix products  22.9 us (5%)
  between operations  14.5 us (3%)
  other arithmetic  8.97 us (2%)
    psum x1, waiting for transfers between devices, broadcast(): return lax.psum(block, axis)  266 us
    reduce_scatter x2, waiting for transfers between devices, on_device(): lax.psum_scatter(step_term(jnp.int32(0), share_rows * lax.axis_size('tm')...  142 us
    unnamed x36, local copies, waits for them, and re-layouts  27.6 us
    dot_general x2, matrix products, lag_products(): lax.dot_general(source_rows, receiver_rows, (((1,), (1,)), ((), ())), pre...  22.9 us
  transfers between devices with their start and end apart: 3, of which 3 were waited for; matrix products, arithmetic and copies ran while one was open for 5% of the time, Pallas kernels for 0%

commit v1 on v0

--- a/solution.py
+++ b/solution.py
@@ -13,7 +13,12 @@
 
 def broadcast(block, axis, owner):
     block = jnp.where(lax.axis_index(axis) == owner, block, jnp.zeros_like(block))
-    return lax.psum(block, axis)
+
+    def mix_local_data(mat):
+        tile_out = lax.all_gather(mat, axis_name=axis)
+        return jnp.sum(tile_out, axis=0)
+
+    return mix_local_data(block)
 
 
 def whiten(records, quality):

time: 486 us -> 419 us (0.86)
  waiting for transfers between devices: 408 us -> 340 us
  other arithmetic: 8.97 us -> 23.1 us
  local copies, waits for them, and re-layouts: 31.1 us -> 20.9 us
    psum x1 -> x0, waiting for transfers between devices: 266 us -> none  [broadcast(): return lax.psum(block, axis)]
    all_gather x0 -> x2, waiting for transfers between devices: none -> 205 us  [mix_local_data(): tile_out = lax.all_gather(mat, axis_name=axis)]
    reduce_sum x0 -> x2, other arithmetic: none -> 15.3 us  [mix_local_data(): return jnp.sum(tile_out, axis=0)]
    unnamed x36 -> x30, local copies, waits for them, and re-layouts: 27.6 us -> 15.3 us
    reduce_scatter x2, waiting for transfers between devices: 142 us -> 135 us  [on_device(): lax.psum_scatter(step_term(jnp.int32(0), share_rows * lax.axis_size('tm')...]
  transfers between devices with their start and end apart: 3 -> 4, of which waited for: 3 -> 4; matrix products, arithmetic and copies ran while one was open for 5% -> 13% of each run, Pallas kernels for 0% -> 0%
where the time goes in v1:
time: 419 us; the launch traced here: 418 us
  waiting for transfers between devices  340 us (81%)
  other arithmetic  23.1 us (6%)
  local copies, waits for them, and re-layouts  20.9 us (5%)
  matrix products  19.7 us (5%)
  between operations  14.7 us (4%)
    all_gather x2, waiting for transfers between devices, mix_local_data(): tile_out = lax.all_gather(mat, axis_name=axis)  205 us
    reduce_scatter x2, waiting for transfers between devices, on_device(): lax.psum_scatter(step_term(jnp.int32(0), share_rows * lax.axis_size('tm')...  135 us
    dot_general x2, matrix products, lag_products(): lax.dot_general(source_rows, receiver_rows, (((1,), (1,)), ((), ())), pre...  19.7 us
    unnamed x30, local copies, waits for them, and re-layouts  15.3 us
    reduce_sum x2, other arithmetic, mix_local_data(): return jnp.sum(tile_out, axis=0)  15.3 us
  transfers between devices with their start and end apart: 4, of which 4 were waited for; matrix products, arithmetic and copies ran while one was open for 13% of the time, Pallas kernels for 0%

profile of v1, /device:TPU:1, one launch (start us, length us, event | category | flops | bytes accessed | tf_op | source)
XLA Modules:
  0.0 418.4 jit_solution(12007948197085296933)
XLA Ops:
  6.5 0.0 all-gather.7.cloned.1.call-start
  6.5 1.4 fusion.16
  9.3 1.9 copy.10
  11.2 0.7 convert_element_type.45
  11.9 0.2 multiply_reduce_fusion
  12.0 0.2 multiply_convert_fusion
  12.2 0.6 dynamic-slice_select_fusion.1
  12.8 1.0 copy.13
  13.8 0.0 all-gather.7.cloned.1.call-update
  13.8 0.0 all-gather.5.cloned.1.call-start
  13.9 1.0 copy.11
  14.9 0.0 all-gather.5.cloned.1.call-update
  14.9 0.0 reduce-scatter.5.cloned.1.call-start
  15.0 1.1 bitcast_dynamic-update-slice_fusion.9
  16.1 1.1 bitcast_dynamic-update-slice_fusion.8
  17.2 1.1 bitcast_dynamic-update-slice_fusion.7
  18.3 1.1 bitcast_dynamic-update-slice_fusion.6
  19.4 1.1 bitcast_dynamic-update-slice_fusion.5
  20.5 1.1 bitcast_dynamic-update-slice_fusion.4
  21.6 1.0 bitcast_dynamic-update-slice_fusion.3
  22.6 1.1 bitcast_dynamic-update-slice_fusion.2
  23.7 1.1 bitcast_dynamic-update-slice_fusion.1
  24.8 1.1 bitcast_dynamic-update-slice_fusion
  25.9 109.6 %all-gather.7.cloned.1.call-done = bf16[2048,3,1024]{2,0,1:T(8,128)(2,1)} async-done(((bf16[64,3,1024]{2,0,1:T(8,128)(2,1)}), bf16[2048,3,1024]{2,0,1:T(8,128)(2,1)}) %all-gather.7.cloned.1.call-update) | async-done | bytes 12582928 | tf_op jit(solution)/shard_map/all_gather | solution.py:18
  135.5 7.6 %reduce_sum.35 = bf16[64,3,1024]{2,0,1:T(8,128)(2,1)S(1)} reduce(bf16[32,64,3,1024]{3,1,0,2:T(8,128)(2,1)} %bitcast.111, bf16[]{:T(256)} %constant.47.clone.1), dimensions={0}, to_apply=%region_3.4 | reduce | flops 6094848 | bytes 12976130 | tf_op jit(solution)/shard_map/reduce_sum | solution.py:19
  143.2 0.2 bitcast_dynamic-update-slice_fusion.19
  143.4 0.2 bitcast_dynamic-update-slice_fusion.18
  143.6 0.2 bitcast_dynamic-update-slice_fusion.17
  143.8 0.2 bitcast_dynamic-update-slice_fusion.16
  144.0 0.2 bitcast_dynamic-update-slice_fusion.15
  144.2 0.2 bitcast_dynamic-update-slice_fusion.14
  144.4 0.2 bitcast_dynamic-update-slice_fusion.13
  144.6 0.2 bitcast_dynamic-update-slice_fusion.12
  144.8 0.2 bitcast_dynamic-update-slice_fusion.11
  145.0 0.2 bitcast_dynamic-update-slice_fusion.10
  145.2 9.8 %fusion.11 = f32[64,10,11,128]{3,0,1,2:T(8,128)S(1)} fusion(bf16[128,10,3,1035]{0,3,2,1:T(8,128)(2,1)} %bitcast_dynamic-update-slice_fusion, bf16[64,11,3,1035]{3,0,2,1:T(8,128)(2,1)S(1)} %bitcast_dynamic-update-slice_fusion.10), kind=kOutput, calls=%fused_computation.9 | convolution fusion | flops 5595955200 | bytes 15925120 | tf_op jit(solution)/shard_map/dot_general | solution.py:69
  155.0 0.4 copy.14
  155.5 2.1 slice_multiply_fusion
  157.6 0.0 reduce-scatter.5.cloned.1.call-update
  157.6 0.0 reduce-scatter.3.cloned.1.call-start
  157.6 95.2 %all-gather.5.cloned.1.call-done = bf16[2048,3,1024]{2,0,1:T(8,128)(2,1)} async-done(((bf16[64,3,1024]{2,0,1:T(8,128)(2,1)}), bf16[2048,3,1024]{2,0,1:T(8,128)(2,1)}) %all-gather.5.cloned.1.call-update) | async-done | bytes 12582928 | tf_op jit(solution)/shard_map/all_gather | solution.py:18
  252.8 7.6 %reduce_sum.34 = bf16[64,3,1024]{2,0,1:T(8,128)(2,1)S(1)} reduce(bf16[32,64,3,1024]{3,1,0,2:T(8,128)(2,1)} %bitcast.110, bf16[]{:T(256)} %constant.47.clone.1), dimensions={0}, to_apply=%region_1.2 | reduce | flops 6094848 | bytes 12976130 | tf_op jit(solution)/shard_map/reduce_sum | solution.py:19
  260.5 0.2 bitcast_dynamic-update-slice_fusion.30
  260.7 0.2 bitcast_dynamic-update-slice_fusion.29
  260.9 0.2 bitcast_dynamic-update-slice_fusion.28
  261.1 0.2 bitcast_dynamic-update-slice_fusion.27
  261.3 0.2 bitcast_dynamic-update-slice_fusion.26
  261.5 0.2 bitcast_dynamic-update-slice_fusion.25
  261.7 0.2 bitcast_dynamic-update-slice_fusion.24
  261.9 0.2 bitcast_dynamic-update-slice_fusion.23
  262.1 0.2 bitcast_dynamic-update-slice_fusion.22
  262.3 0.2 bitcast_dynamic-update-slice_fusion.21
  262.5 9.9 %fusion.6 = f32[64,10,11,128]{3,0,1,2:T(8,128)S(1)} fusion(bf16[128,10,3,1035]{0,3,2,1:T(8,128)(2,1)} %bitcast_dynamic-update-slice_fusion, bf16[64,11,3,1035]{3,0,2,1:T(8,128)(2,1)S(1)} %bitcast_dynamic-update-slice_fusion.21), kind=kOutput, calls=%fused_computation.8 | convolution fusion | flops 5595955200 | bytes 15925120 | tf_op jit(solution)/shard_map/dot_general | solution.py:69
  272.3 0.3 copy.12
  272.6 2.1 slice_multiply_fusion.1
  274.7 0.0 reduce-scatter.3.cloned.1.call-update
  274.7 55.0 %reduce-scatter.5.cloned.1.call-done = f32[8,101,128]{2,0,1:T(8,128)} async-done(((f32[64,101,128]{2,0,1:T(8,128)}), f32[8,101,128]{2,0,1:T(8,128)}) %reduce-scatter.5.cloned.1.call-update) | async-done | bytes 413712 | tf_op jit(solution)/shard_map/reduce_scatter | solution.py:104
  329.7 80.1 %reduce-scatter.3.cloned.1.call-done = f32[8,101,128]{2,0,1:T(8,128)} async-done(((f32[64,101,128]{2,0,1:T(8,128)}), f32[8,101,128]{2,0,1:T(8,128)}) %reduce-scatter.3.cloned.1.call-update) | async-done | bytes 413712 | tf_op jit(solution)/shard_map/reduce_scatter | solution.py:104
  409.8 2.1 pad_maximum_fusion
  (3 shorter events, 0.1 us)
Async XLA Ops:
  6.5 129.0 %all-gather.7.cloned.1.call-start = ((), (), s32[]{:S(2)}) async-start(), calls=%async_computation.5 | async-start | bytes 12976128 | tf_op jit(solution)/shard_map/all_gather | solution.py:18
  13.8 238.9 %all-gather.5.cloned.1.call-start = ((), (), s32[]{:S(2)}) async-start(), calls=%async_computation.4 | async-start | bytes 12976128 | tf_op jit(solution)/shard_map/all_gather | solution.py:18
  14.9 314.8 %reduce-scatter.5.cloned.1.call-start = ((), (), s32[]{:S(2)}) async-start(), calls=%async_computation.3 | async-start | bytes 3723264 | tf_op jit(solution)/shard_map/reduce_scatter | solution.py:104
  157.6 252.2 %reduce-scatter.3.cloned.1.call-start = ((), (), s32[]{:S(2)}) async-start(), calls=%async_computation.2 | async-start | bytes 3723264 | tf_op jit(solution)/shard_map/reduce_scatter | solution.py:104
Sparse Core Ops, SparseCore 0:
  14.0 121.4 all-gather.6
  138.3 114.4 all-gather.4
  255.4 74.2 reduce-scatter.4
  332.1 77.6 reduce-scatter.2
